TPU v7x, 256 devices: a whole 4x4x8 slice. The times are simulated.
256 devices in a mesh: pair: 16 (over z, x_lo), side: 2 (over core), tp: 8 (over y, x_hi).
Axes of the slice: x: 4 (x_hi: 2, x_lo: 2; x = x_hi * 2 + x_lo), y: 4, z: 8, core: 2. Of those that a mesh axis runs over, the one named last changes fastest.
Arguments:
- segment_queries: bfloat16 [16, 1024, 8192], P('pair', 'side', 'tp'), may hold values from -60 to 60
- segment_kv: bfloat16 [16, 1024, 2048], P('pair', 'side', 'tp'), may hold values from -6 to 6
- prefix_kv: bfloat16 [16, 1024, 2048], P('pair', None, 'tp'), may hold values from -8 to 8
- kv_cache: bfloat16 [16, 7, 2048, 2048], P('pair', None, ('side', 'tp')), may hold values from -8 to 8
- decode_queries: bfloat16 [16, 4, 8, 8192], P('pair'), may hold values from -60 to 60
- decode_kv: bfloat16 [16, 4, 8, 2048], P('pair'), may hold values from -6 to 6
- matching: int32 [16], replicated, may hold values from 0 to 15, each once
- segment_starts: int32 [16], replicated, may hold values from 2 to 1024, as said below
- cache_lengths: int32 [16, 7], P('pair'), may hold values from 2 to 2048, as said below
Outputs:
- prompt_out: bfloat16 [16, 1024, 8192], P('pair', 'side', 'tp')
- decode_out: bfloat16 [16, 4, 8, 8192], P('pair', None, None, ('side', 'tp'))
Inputs may be any that keep to these rules, and one draw needn't show every extreme that they name: `matching`: each group index appears once. `segment_starts`: the largest entry equals 1024. `cache_lengths`: the largest entry equals 2048.
All inputs are finite; a program needn't handle non-finite values.
Results may differ from a plain program's by a relative error of at most 0.0075.
Values may be sent and summed in bfloat16 or wider, within the bound.
No kernel may reach another device: no remote copies, remote signals or barrier semaphores. Data moves between devices by JAX's collectives and lax.ppermute only.
A program may use at most 128 MiB of HBM per device.

v0:
```python
import math

import jax
import jax.numpy as jnp
from jax import lax
from jax.sharding import PartitionSpec as P

H = 64
KVH = 8
HD = 128
PREFIX = 1024


NEG_FILL = -1e30


def from_behind(value, axis, by):
    peers = lax.axis_size(axis)
    pairs = [(i, i + by) for i in range(peers) if 0 <= i + by < peers]
    return lax.ppermute(value, axis, pairs)


def softmax_parts(scores, allowed, highest):
    weights = jnp.where(allowed, jnp.exp(scores - highest), 0.0)
    return (weights.astype(jnp.bfloat16), jnp.sum(weights, axis=-1))


def prompt_block(queries, keys_all, allowed, factor):
    scores = (
        jnp.einsum("qcgd,jcd->qcgj", queries, keys_all[:, :, 0], preferred_element_type=jnp.float32)
        * factor
    )
    scores = jnp.where(allowed, scores, NEG_FILL)
    highest = jnp.max(scores, axis=-1, keepdims=True)
    rounded, totals = softmax_parts(scores, allowed, highest)
    mixture = jnp.einsum(
        "qcgj,jcd->qcgd", rounded, keys_all[:, :, 1], preferred_element_type=jnp.float32
    )
    return (mixture / totals[..., None]).astype(jnp.bfloat16)


def row_scores(queries, keys_kv, allowed, fresh_kv, causal, factor):
    key_count = keys_kv.shape[0]
    steps_total = queries.shape[0]
    joined = jnp.concatenate([keys_kv, fresh_kv], axis=0).reshape(
        key_count + steps_total, -1, 2, HD
    )
    allowed_all = jnp.concatenate(
        [jnp.broadcast_to(allowed[None, :], (steps_total, key_count)), causal], axis=1
    )[:, None, None, :]
    grouped = queries.reshape(steps_total, joined.shape[1], H // KVH, HD)
    scores = (
        jnp.einsum("scgd,jcd->scgj", grouped, joined[:, :, 0], preferred_element_type=jnp.float32)
        * factor
    )
    return (jnp.where(allowed_all, scores, NEG_FILL), allowed_all, joined[:, :, 1])


def row_mix(scores, allowed_all, values_kv, highest):
    rounded, totals = softmax_parts(scores, allowed_all, highest[..., None])
    mixture = jnp.einsum("scgj,jcd->scgd", rounded, values_kv, preferred_element_type=jnp.float32)
    return (totals, mixture)


def local(
    segment_queries,
    segment_kv,
    prefix_kv,
    kv_cache,
    decode_queries,
    decode_kv,
    matching,
    segment_starts,
    cache_lengths,
):
    factor = 1.0 / math.sqrt(HD)
    group_id = lax.axis_index("pair")
    side_id = lax.axis_index("side")
    tp_id = lax.axis_index("tp")
    tp_size = lax.axis_size("tp")
    side_size = lax.axis_size("side")
    block_id = side_id * tp_size + tp_id
    own_queries = segment_queries[0]
    own_kv = segment_kv[0]
    prefix = prefix_kv[0]
    half_len = own_kv.shape[0]
    kv_cols = own_kv.shape[1]
    kv_heads = kv_cols // (2 * HD)
    per_kv = H // KVH
    earlier = from_behind(own_kv, "side", 1)
    first_new = segment_starts[group_id]
    keys_all = jnp.concatenate([prefix, earlier, own_kv], axis=0).reshape(
        PREFIX + 2 * half_len, kv_heads, 2, HD
    )
    key_pos = jnp.arange(PREFIX + 2 * half_len, dtype=jnp.int32)
    block_rows = min(256, half_len)

    def prompt_rows(block_index):
        row_start = block_index * block_rows
        query_pos = row_start + jnp.arange(block_rows, dtype=jnp.int32)
        allowed = jnp.where(
            key_pos[None, :] < PREFIX,
            key_pos[None, :] < first_new,
            jnp.where(
                key_pos[None, :] < PREFIX + half_len,
                side_id > 0,
                key_pos[None, :] - PREFIX - half_len <= query_pos[:, None],
            ),
        )
        queries = lax.dynamic_slice_in_dim(own_queries, row_start, block_rows, 0).reshape(
            block_rows, kv_heads, per_kv, HD
        )
        return prompt_block(queries, keys_all, allowed[:, None, None, :], factor).reshape(
            block_rows, kv_heads * per_kv * HD
        )

    prompt_out = lax.map(prompt_rows, jnp.arange(half_len // block_rows, dtype=jnp.int32)).reshape(
        1, half_len, -1
    )
    prefix_share = PREFIX // side_size
    prefix_part = lax.dynamic_slice_in_dim(prefix, side_id * prefix_share, prefix_share, 0)
    group_ids = jnp.arange(matching.shape[0], dtype=jnp.int32)
    inverse = jnp.sum(
        jnp.where(matching[:, None] == group_ids[None, :], group_ids[:, None], 0), axis=0
    )
    source = inverse[group_id]
    source_start = segment_starts[source]
    queries_all = decode_queries[0]
    fresh_all = decode_kv[0]
    steps_total = queries_all.shape[0]
    step_ids = jnp.arange(steps_total, dtype=jnp.int32)
    step_causal = step_ids[None, :] <= step_ids[:, None]
    causal = step_causal & (block_id == 0)
    phased = jnp.concatenate(
        [
            prefix_part.reshape(tp_size, prefix_share // tp_size, kv_cols),
            own_kv.reshape(tp_size, half_len // tp_size, kv_cols),
        ],
        axis=1,
    ).reshape(-1, kv_cols)
    blocks_kv = lax.all_to_all(phased, "tp", split_axis=0, concat_axis=1, tiled=True)
    pieces = lax.all_gather(blocks_kv[None], "pair", axis=0, tiled=True)
    owners = jnp.arange(pieces.shape[0], dtype=jnp.int32)
    picked = jnp.where((owners == source)[:, None, None], pieces, jnp.zeros_like(pieces))
    received = jnp.sum(picked, axis=0)
    prefix_block = PREFIX // (side_size * tp_size)
    segment_block = half_len // tp_size
    first_allowed = jnp.concatenate(
        [
            block_id * prefix_block + jnp.arange(prefix_block, dtype=jnp.int32) < source_start,
            jnp.ones((segment_block,), jnp.bool_),
        ]
    )
    first_queries = queries_all[:, 0]
    first_fresh = fresh_all[:, 0]
    cache_rows = kv_cache[0]
    cache_len = cache_rows.shape[1]
    cache_allowed = (block_id * cache_len + jnp.arange(cache_len, dtype=jnp.int32))[
        None, :
    ] < cache_lengths[0][:, None]
    first_scores, first_mask, first_values = row_scores(
        first_queries, received, first_allowed, first_fresh, causal, factor
    )

    def running_scores(row_queries, row_cache, row_allowed, row_fresh):
        return row_scores(row_queries, row_cache, row_allowed, row_fresh, causal, factor)

    rest_scores, rest_mask, rest_values = jax.vmap(running_scores, in_axes=(1, 0, 0, 1))(
        queries_all[:, 1:], cache_rows, cache_allowed, fresh_all[:, 1:]
    )
    first_peak = jnp.max(first_scores, axis=-1)
    local_peak = jnp.concatenate(
        [first_peak[:, None], jnp.transpose(jnp.max(rest_scores, axis=-1), (1, 0, 2, 3))], axis=1
    )
    heads_dev = H // (side_size * tp_size)
    highest = lax.pmax(local_peak, ("side", "tp"))
    first_high = highest[:, 0]
    first_totals, first_mix = row_mix(first_scores, first_mask, first_values, first_high)
    rest_totals, rest_mix = jax.vmap(row_mix, in_axes=(0, 0, 0, 1))(
        rest_scores, rest_mask, rest_values, highest[:, 1:]
    )
    totals = jnp.concatenate(
        [first_totals[:, None], jnp.transpose(rest_totals, (1, 0, 2, 3))], axis=1
    )
    mixture = jnp.concatenate(
        [first_mix[:, None], jnp.transpose(rest_mix, (1, 0, 2, 3, 4))], axis=1
    )
    rows_total = totals.shape[1]
    totals, mixture = (
        totals.reshape(steps_total, rows_total, H),
        mixture.reshape(steps_total, rows_total, H * HD),
    )
    totals, mixture = lax.psum((totals, mixture), ("side", "tp"))
    totals = lax.dynamic_slice_in_dim(totals, block_id * heads_dev, heads_dev, 2)
    mixture = lax.dynamic_slice_in_dim(
        mixture.reshape(steps_total, -1, H, HD), block_id * heads_dev, heads_dev, 2
    )
    decode_out = (
        (mixture / totals[..., None])
        .astype(jnp.bfloat16)
        .reshape(1, steps_total, -1, heads_dev * HD)
    )
    return (prompt_out, decode_out)


def solution(mesh):
    in_specs = (
        P("pair", "side", "tp"),
        P("pair", "side", "tp"),
        P("pair", None, "tp"),
        P("pair", None, ("side", "tp"), None),
        P("pair", None, None, None),
        P("pair", None, None, None),
        P(),
        P(),
        P("pair", None),
    )
    out_specs = (P("pair", "side", "tp"), P("pair", None, None, ("side", "tp")))
    return jax.shard_map(local, mesh=mesh, in_specs=in_specs, out_specs=out_specs, check_vma=False)
```

profile of v0, /device:TPU:57, one launch (start us, length us, event | category | flops | bytes accessed | tf_op | source)
XLA Modules:
  0.0 453.4 jit_solution(1956947212354036460)
XLA Ops:
  7.2 1.0 constant_dynamic-slice_fusion.1
  8.3 1.0 pad_maximum_fusion.3
  9.3 15.0 %all_to_all.13 = bf16[8,128,256]{2,1,0:T(8,128)(2,1)S(1)} all-to-all(bf16[8,128,256]{2,1,0:T(8,128)(2,1)S(1)} %pad_maximum_fusion.3), channel_id=1, replica_groups=mesh['pair'=16,'side'=2,'tp'=8] {'tp'}, dimensions={0} | all-to-all | bytes 1048576 | tf_op jit(solution)/shard_map/all_to_all | solution.py:141
  24.3 0.3 copy.134
  24.5 1.0 copy.135
  25.6 0.1 copy.130
  25.8 1.3 collective-permute-start
  27.2 0.6 dynamic_slice.38
  29.1 0.1 reshape.271
  29.3 6.1 %copy.140 = bf16[1,7,128,2048]{2,3,1,0:T(8,128)(2,1)} copy(bf16[1,7,128,2048]{3,2,1,0:T(8,128)(2,1)} %param.14) | data formatting | bytes 7340032 | tf_op args[3]
  35.4 6.1 %copy.142 = bf16[7,128,8,2,128]{4,1,2,0,3:T(8,128)(2,1)} copy(bf16[7,128,8,2,128]{1,4,3,2,0:T(8,128)(2,1)} %bitcast.178) | data formatting | bytes 7340032 | tf_op jit(solution)/shard_map/vmap()/concatenate | solution.py:45
  41.5 0.1 slice_bitcast_fusion.2
  41.6 0.6 reshape.272
  42.9 0.6 fusion.66
  43.5 0.6 iota_compare_fusion.5
  44.2 0.7 add_compare_fusion
  45.1 0.4 slice_reduce_fusion
  45.5 4.9 %fusion.28 = (f32[7,4,8,8]{3,1,2,0:T(4,128)}, f32[7,8,132,4,8]{2,4,3,1,0:T(8,128)}) fusion(pred[7,4,132]{2,1,0:T(4,128)(4,1)S(1)} %pad_add_fusion, bf16[7,4,8,8,128]{4,3,2,0,1:T(8,128)(2,1)S(1)} %reshape.272, bf16[7,128,8,2,128]{4,1,2,0,3:T(8,128)(2,1)} %copy.142, bf16[7,4,8,2,128]{4,1,2,0,3:T(4,128)(2,1)S(1)} %copy.143), kind=kOutput, calls=%fused_computation.38 | convolution fusion | flops 65047808 | bytes 5200496 | tf_op jit(solution)/shard_map/vmap(scgd,jcd->scgj)/dot_general | solution.py:53
  50.4 0.2 copy.129
  50.6 1.3 copy.128
  52.1 0.1 pad_maximum_fusion.1
  52.2 0.7 copy.132
  52.9 157.0 %all-gather.2.cloned.1.call-done = bf16[16,128,2048]{2,1,0:T(8,128)(2,1)} async-done(((bf16[1,128,2048]{2,1,0:T(8,128)(2,1)}), bf16[16,128,2048]{2,1,0:T(8,128)(2,1)}) %all-gather.2.cloned.1.call-update) | async-done | bytes 8388624 | tf_op jit(solution)/shard_map/all_gather | solution.py:142
  209.9 5.6 %select_reduce_fusion = bf16[128,2048]{1,0:T(8,128)(2,1)S(1)} fusion(bf16[16,128,2048]{2,1,0:T(8,128)(2,1)} %all-gather.2.cloned.1.call-done, pred[16]{0:T(512)(128)(4,1)S(1)} %iota_compare_fusion.5), kind=kLoop, calls=%fused_computation.26 | loop fusion | flops 8126464 | bytes 8912912 | tf_op jit(solution)/shard_map/reduce_sum | solution.py:145
  215.4 0.3 copy.136
  215.7 0.3 copy.137
  216.0 1.0 fusion.67
  217.1 69.0 %pmax.7 = f32[4,8,8,8]{3,0,2,1:T(4,128)S(1)} all-reduce(f32[4,8,8,8]{3,0,2,1:T(4,128)S(1)} %pad_maximum_fusion.5), channel_id=1, replica_groups=mesh['pair'=16,'side'=2,'tp'=8] {'side','tp'}, use_global_device_ids=true, to_apply=%region_8.9 | all-reduce | flops 2048 | bytes 16384 | tf_op jit(solution)/shard_map/pmax | solution.py:176
  286.1 2.8 fusion.29
  289.0 0.1 copy.147
  289.1 0.4 concatenate.73
  289.5 1.2 convolution_bitcast_fusion
  290.7 0.3 pad_maximum_fusion.2
  291.0 1.7 reshape.255
  292.7 0.5 iota.51
  293.3 57.6 %while.16 = (s32[]{:T(128)}, bf16[2,256,1024]{2,1,0:T(8,128)(2,1)}, s32[]{:T(128)}, pred[]{:T(512)}, s32[2]{0:T(128)}, /*index=5*/bf16[512,1024]{0,1:T(8,128)(2,...) while((s32[]{:T(128)}, bf16[2,256,1024]{2,1,0:T(8,128)(2,1)}, ...), condition=%wide.region_3.4_spmd.clone.clone, body=%wide.region_0.3_spmd.clone.clone.sunk | while | flops 2204111104 | bytes 126949600 | solution.py:117
  293.3 1.4 dynamic_slice.58
  295.4 0.6 iota_compare_fusion.8
  295.9 0.6 select_select_fusion.2
  296.5 1.1 constant_dynamic-slice_fusion.4
  297.6 7.5 %fusion.75 = (f32[256,8]{0,1:T(8,128)S(1)}, f32[256,8,2048]{2,0,1:T(8,128)}) fusion(pred[256,2048]{1,0:T(8,128)(4,1)S(1)} %select_select_fusion.2, bf16[256,8,128]{0,2,1:T(8,128)(2,1)S(1)} %bitcast.177, bf16[2048,1,2,128]{3,0,2,1:T(8,128)(2,1)S(1)} %get-tuple-element.358), kind=kOutput, calls=%fused_computation.3.clone.1 | convolution fusion | flops 1086322688 | bytes 18358272 | tf_op jit(solution)/shard_map/while/body/eval_jaxpr/qcgd,jcd->qcgj/dot_general | solution.py:30
  305.1 0.5 copy.179
  305.6 8.8 %fusion.76 = f32[256,8]{0,1:T(8,128)S(1)} fusion(f32[256,8,2048]{2,0,1:T(8,128)} %get-tuple-element.328, f32[256,8]{0,1:T(8,128)S(1)} %get-tuple-element.329, pred[256,2048]{1,0:T(8,128)(4,1)S(1)} %select_select_fusion.2), kind=kLoop, calls=%fused_computation.4.clone.1 | loop fusion | flops 20969472 | bytes 17317888 | tf_op jit(solution)/shard_map/while/body/eval_jaxpr/reduce_sum | solution.py:25
  314.4 1.9 copy-done
  316.3 4.7 %divide_convert_fusion.2 = bf16[1,128,256,8]{2,1,3,0:T(8,128)(2,1)S(1)} fusion(f32[256,8,2048]{2,0,1:T(8,128)S(1)} %copy-done, f32[256,8]{0,1:T(8,128)S(1)} %get-tuple-element.329, pred[256,2048]{1,0:T(8,128)(4,1)S(1)} %select_select_fusion.2, bf16[2048,1,2,128]{0,3,2,1:T(8,128)(2,1)S(1)} %copy.179, f32[256,8]{0,1:T(8,128)S(1)} %fusion.76), kind=kOutput, calls=%fused_computation.11.clone.1 | convolution fusion | flops 1095237632 | bytes 18366464 | tf_op jit(solution)/shard_map/while/body/eval_jaxpr/qcgj,jcd->qcgd/dot_general | solution.py:36
  321.0 0.2 copy.180
  321.2 0.8 constant_dynamic-update-slice_fusion.2
  322.1 1.3 dynamic_slice.58
  324.1 0.6 iota_compare_fusion.8
  324.7 0.6 select_select_fusion.2
  325.3 1.1 constant_dynamic-slice_fusion.4
  326.4 7.4 %fusion.75 = (f32[256,8]{0,1:T(8,128)S(1)}, f32[256,8,2048]{2,0,1:T(8,128)}) fusion(pred[256,2048]{1,0:T(8,128)(4,1)S(1)} %select_select_fusion.2, bf16[256,8,128]{0,2,1:T(8,128)(2,1)S(1)} %bitcast.177, bf16[2048,1,2,128]{3,0,2,1:T(8,128)(2,1)S(1)} %get-tuple-element.358), kind=kOutput, calls=%fused_computation.3.clone.1 | convolution fusion | flops 1086322688 | bytes 18358272 | tf_op jit(solution)/shard_map/while/body/eval_jaxpr/qcgd,jcd->qcgj/dot_general | solution.py:30
  333.8 0.5 copy.179
  334.3 8.8 %fusion.76 = f32[256,8]{0,1:T(8,128)S(1)} fusion(f32[256,8,2048]{2,0,1:T(8,128)} %get-tuple-element.328, f32[256,8]{0,1:T(8,128)S(1)} %get-tuple-element.329, pred[256,2048]{1,0:T(8,128)(4,1)S(1)} %select_select_fusion.2), kind=kLoop, calls=%fused_computation.4.clone.1 | loop fusion | flops 20969472 | bytes 17317888 | tf_op jit(solution)/shard_map/while/body/eval_jaxpr/reduce_sum | solution.py:25
  343.1 1.9 copy-done
  345.0 4.7 %divide_convert_fusion.2 = bf16[1,128,256,8]{2,1,3,0:T(8,128)(2,1)S(1)} fusion(f32[256,8,2048]{2,0,1:T(8,128)S(1)} %copy-done, f32[256,8]{0,1:T(8,128)S(1)} %get-tuple-element.329, pred[256,2048]{1,0:T(8,128)(4,1)S(1)} %select_select_fusion.2, bf16[2048,1,2,128]{0,3,2,1:T(8,128)(2,1)S(1)} %copy.179, f32[256,8]{0,1:T(8,128)S(1)} %fusion.76), kind=kOutput, calls=%fused_computation.11.clone.1 | convolution fusion | flops 1095237632 | bytes 18366464 | tf_op jit(solution)/shard_map/while/body/eval_jaxpr/qcgj,jcd->qcgd/dot_general | solution.py:36
  349.8 0.2 copy.180
  350.0 0.8 constant_dynamic-update-slice_fusion.2
  350.8 2.3 fusion.32
  353.3 0.9 fusion.49
  354.3 65.3 %psum.15 = f32[4,8,64]{2,0,1:T(4,128)S(1)} all-reduce(f32[4,8,64]{2,0,1:T(4,128)S(1)} %pad_maximum_fusion.6), channel_id=1, replica_groups=mesh['pair'=16,'side'=2,'tp'=8] {'side','tp'}, use_global_device_ids=true, to_apply=%region_12.13 | all-reduce | flops 2048 | bytes 16384 | tf_op jit(solution)/shard_map/psum | solution.py:193
  419.7 25.2 %all-reduce.3.cloned.1.call-done = f32[4,8,64,128]{3,2,0,1:T(8,128)} async-done(((f32[4,8,64,128]{3,2,0,1:T(8,128)}), f32[4,8,64,128]{3,2,0,1:T(8,128)}) %all-reduce.3.cloned.1.call-update) | async-done | bytes 1048592 | tf_op jit(solution)/shard_map/psum | solution.py:193
  444.9 1.0 fusion.56
  445.9 0.6 copy.176
  (73 shorter events, 1.0 us)
Async XLA Ops:
  7.2 18.4 %copy-start.3 = (bf16[1,512,256]{2,1,0:T(8,128)(2,1)S(1)}, bf16[1,512,256]{2,1,0:T(8,128)(2,1)}, u32[]{:S(2)}) copy-start(bf16[1,512,256]{2,1,0:T(8,128)(2,1)} %param.12) | copy-start | bytes 786436
  7.2 19.9 %copy-start.17 = (s32[16]{0:T(128)S(1)}, s32[16]{0:T(128)}, u32[]{:S(2)}) copy-start(s32[16]{0:T(128)} %param.17) | copy-start | bytes 196
  7.2 21.9 %copy-start.8 = (bf16[1,4,8,2048]{3,2,1,0:T(8,128)(2,1)S(1)}, bf16[1,4,8,2048]{3,2,1,0:T(8,128)(2,1)}, u32[]{:S(2)}) copy-start(bf16[1,4,8,2048]{3,2,1,0:T(8,128)(2,1)} %param.16) | copy-start | bytes 393220
  7.2 202.7 %all-gather.2.cloned.1.call-start = ((), (), s32[]{:S(2)}) async-start(), calls=%async_computation.1 | async-start | bytes 8912896 | tf_op jit(solution)/shard_map/all_gather | solution.py:142
  25.6 419.3 %all-reduce.3.cloned.1.call-start = ((), (), s32[]{:S(2)}) async-start(), calls=%async_computation.2 | async-start | bytes 2097152 | tf_op jit(solution)/shard_map/psum | solution.py:193
  25.8 26.3 %collective-permute-start = (bf16[512,256]{0,1:T(8,128)(2,1)S(1)}, bf16[512,256]{0,1:T(8,128)(2,1)S(1)}, u32[]{:S(2)}, u32[]{:S(2)}) collective-permute-start(bf16[512,256]{0,1:T(8,128)(2,1)S(1)} %bitcast.186), channel_id=1, source_target_pairs={{0,8},{1,9},{2,10},{3,11},{4,12},{5,13},{6,14},{7,15},{16,24},{17,... | collective-permute-start | bytes 786440 | tf_op jit(solution)/shard_map/ppermute | solution.py:20
  29.3 16.2 %copy-start.9 = (bf16[7,4,8,2,128]{4,1,2,0,3:T(4,128)(2,1)}, bf16[7,4,8,2,128]{4,1,2,0,3:T(4,128)(2,1)S(1)}, u32[]{:S(2)}) copy-start(bf16[7,4,8,2,128]{4,1,2,0,3:T(4,128)(2,1)S(1)} %copy.143) | copy-start | bytes 344068
  35.4 6.1 %copy-start.5 = (bf16[1,4,8,8192]{3,2,1,0:T(8,128)(2,1)S(1)}, bf16[1,4,8,8192]{3,2,1,0:T(8,128)(2,1)}, u32[]{:S(2)}) copy-start(bf16[1,4,8,8192]{3,2,1,0:T(8,128)(2,1)} %param.15) | copy-start | bytes 1572868
  35.4 7.5 %copy-start.15 = (s32[16]{0:T(128)S(1)}, s32[16]{0:T(128)}, u32[]{:S(2)}) copy-start(s32[16]{0:T(128)} %param.18) | copy-start | bytes 196
  35.4 9.4 %copy-start.16 = (s32[1,7]{1,0:T(1,128)S(1)}, s32[1,7]{1,0:T(1,128)}, u32[]{:S(2)}) copy-start(s32[1,7]{1,0:T(1,128)} %param.19) | copy-start | bytes 88
  45.0 5.4 %copy-start.12 = (pred[7,4,132]{2,1,0:T(4,128)(4,1)}, pred[7,4,132]{2,1,0:T(4,128)(4,1)S(1)}, u32[]{:S(2)}) copy-start(pred[7,4,132]{2,1,0:T(4,128)(4,1)S(1)} %pad_add_fusion) | copy-start | bytes 11092
  45.5 5.0 %copy-start.1 = (bf16[1,1024,256]{2,1,0:T(8,128)(2,1)S(1)}, bf16[1,1024,256]{2,1,0:T(8,128)(2,1)}, u32[]{:S(2)}) copy-start(bf16[1,1024,256]{2,1,0:T(8,128)(2,1)} %param.13) | copy-start | bytes 1572868
  45.5 5.2 %copy-start.2 = (bf16[1,512,1024]{2,1,0:T(8,128)(2,1)S(1)}, bf16[1,512,1024]{2,1,0:T(8,128)(2,1)}, u32[]{:S(2)}) copy-start(bf16[1,512,1024]{2,1,0:T(8,128)(2,1)} %param.11) | copy-start | bytes 3145732
  52.0 164.0 %copy-start.11 = (bf16[4,8,2,128]{3,0,1,2:T(4,128)(2,1)}, bf16[4,8,2,128]{3,0,1,2:T(4,128)(2,1)S(1)}, u32[]{:S(2)}) copy-start(bf16[4,8,2,128]{3,0,1,2:T(4,128)(2,1)S(1)} %copy.138) | copy-start | bytes 49156
  52.0 164.0 %copy-start.14 = (pred[4,132]{1,0:T(4,128)(4,1)}, pred[4,132]{1,0:T(4,128)(4,1)S(1)}, u32[]{:S(2)}) copy-start(pred[4,132]{1,0:T(4,128)(4,1)S(1)} %pad_add_fusion.1) | copy-start | bytes 1588
  52.8 164.2 %copy-start.10 = (f32[7,4,8,8]{3,1,2,0:T(4,128)S(1)}, f32[7,4,8,8]{3,1,2,0:T(4,128)}, u32[]{:S(2)}) copy-start(f32[7,4,8,8]{3,1,2,0:T(4,128)} %get-tuple-element.275) | copy-start | bytes 21508
  286.1 2.9 copy-start.6
  293.3 57.6 %copy-start.7 = (f32[7,4,8,8]{3,1,2,0:T(4,128)S(1)}, f32[7,4,8,8]{3,1,2,0:T(4,128)}, u32[]{:S(2)}) copy-start(f32[7,4,8,8]{3,1,2,0:T(4,128)} %copy-done.6) | copy-start | bytes 21508
  293.3 57.6 %copy-start.13 = (pred[7,4,132]{2,1,0:T(4,128)(4,1)S(1)}, pred[7,4,132]{2,1,0:T(4,128)(4,1)}, u32[]{:S(2)}) copy-start(pred[7,4,132]{2,1,0:T(4,128)(4,1)} %copy-done.12) | copy-start | bytes 11092
  293.3 60.0 %copy-start.4 = (f32[4,8,8,132]{3,2,0,1:T(8,128)S(1)}, f32[4,8,8,132]{3,2,0,1:T(8,128)}, u32[]{:S(2)}) copy-start(f32[4,8,8,132]{3,2,0,1:T(8,128)} %get-tuple-element.278) | copy-start | bytes 405508
  305.6 10.7 %copy-start = (f32[256,8,2048]{2,0,1:T(8,128)S(1)}, f32[256,8,2048]{2,0,1:T(8,128)}, u32[]{:S(2)}) copy-start(f32[256,8,2048]{2,0,1:T(8,128)} %get-tuple-element.328) | copy-start | bytes 50331652 | tf_op jit(solution)/shard_map/while
  334.3 10.7 %copy-start = (f32[256,8,2048]{2,0,1:T(8,128)S(1)}, f32[256,8,2048]{2,0,1:T(8,128)}, u32[]{:S(2)}) copy-start(f32[256,8,2048]{2,0,1:T(8,128)} %get-tuple-element.328) | copy-start | bytes 50331652 | tf_op jit(solution)/shard_map/while
Sparse Core Ops, SparseCore 0:
  25.7 184.1 all-gather.1
  292.9 151.9 all-reduce.2
where the time goes:
time: 457 us; the launch traced here: 453 us
  waiting for transfers between devices  182 us (40%)
  blocking collectives  149 us (33%)
  local copies, waits for them, and re-layouts  35.6 us (8%)
  matrix products  34.3 us (8%)
  other arithmetic  32.5 us (7%)
  between operations  16.5 us (4%)
    all_gather x1, waiting for transfers between devices, local(): pieces = lax.all_gather(blocks_kv[None], 'pair', axis=0, tiled=True)  157 us
    pmax x1, blocking collectives, local(): highest = lax.pmax(local_peak, ('side', 'tp'))  69 us
    psum x1, blocking collectives, local(): totals, mixture = lax.psum((totals, mixture), ('side', 'tp'))  65.3 us
    psum x1, waiting for transfers between devices, local(): totals, mixture = lax.psum((totals, mixture), ('side', 'tp'))  25.2 us
    reduce_sum x4, other arithmetic, softmax_parts(): return (weights.astype(jnp.bfloat16), jnp.sum(weights, axis=-1))  20.7 us
    all_to_all x1, blocking collectives, local(): lax.all_to_all(phased, 'tp', split_axis=0, concat_axis=1, tiled=True)  15 us
    dot_general x2, matrix products, prompt_block(): jnp.einsum('qcgd,jcd->qcgj', queries, keys_all[:, :, 0], preferred_elemen...  14.9 us
    dot_general x2, matrix products, prompt_block(): jnp.einsum('qcgj,jcd->qcgd', rounded, keys_all[:, :, 1], preferred_elemen...  9.47 us
  transfers between devices with their start and end apart: 3, of which 2 were waited for; matrix products, arithmetic and copies ran while one was open for 18% of the time, Pallas kernels for 0%

commit v1 on v0

v1 whole, which is shorter than its diff:
```python
import functools
import math

import jax
import jax.numpy as jnp
from jax import lax
from jax.experimental import pallas as pl
from jax.experimental.pallas import tpu as pltpu
from jax.sharding import PartitionSpec as P

H = 64
KVH = 8
HD = 128
STEPS = 4
ROWS = 8
GROUPS = 16
BLOCKS = 16
SEG_HALF = 512
PREFIX = 1024
CACHE_BLOCK = 128

FACTOR = 1.0 / math.sqrt(HD)
LOG2E = 1.4426950408889634
NEG_FILL = -1e30
PART_ROWS = 144

f32 = jnp.float32
bf16 = jnp.bfloat16


def params(**kw):
    return pltpu.CompilerParams(vmem_limit_bytes=60 * 1024 * 1024, **kw)


def whole(shape):
    return pl.BlockSpec(shape, lambda *_: (0,) * len(shape))


def dot_t(a, b):
    return lax.dot_general(a, b, (((1,), (1,)), ((), ())), preferred_element_type=f32)


def dot(a, b):
    return jnp.dot(a, b, preferred_element_type=f32)


def prep_kernel(q_ref, kv_ref, out_ref):
    side = lax.axis_index("side")
    tp = lax.axis_index("tp")
    q_col = pl.multiple_of((2 * tp + side) * 512, 512)
    kv_col = pl.multiple_of(tp * 256, 256)
    q = q_ref[0, :, :, pl.ds(q_col, 512)].astype(f32)
    kv = kv_ref[0, :, :, pl.ds(kv_col, 256)].astype(f32)
    rows = [q[t, 0:1, h * HD : (h + 1) * HD] for t in range(STEPS) for h in range(4)]
    pad = [jnp.zeros((4, HD), f32)]
    rows += [kv[u, 0:1, :HD] for u in range(STEPS)] + pad
    rows += [kv[u, 0:1, HD:] for u in range(STEPS)] + pad
    sent = jnp.concatenate(rows, axis=0).astype(bf16)
    for p in range(GROUPS):
        out_ref[p] = sent


def prep(decode_queries, decode_kv):
    shape = (GROUPS, 32, HD)
    return pl.pallas_call(
        prep_kernel,
        out_shape=jax.ShapeDtypeStruct(shape, bf16),
        grid=(1,),
        in_specs=[whole(decode_queries.shape), whole(decode_kv.shape)],
        out_specs=whole(shape),
        compiler_params=params(),
        cost_estimate=pl.CostEstimate(flops=10000, bytes_accessed=800000, transcendentals=0),
        name="prep",
    )(decode_queries, decode_kv)


def decode_kernel(len_ref, q_ref, cache_ref, after_ref, out_ref):
    block = lax.axis_index("side") * 8 + lax.axis_index("tp")
    sub = lax.broadcasted_iota(jnp.int32, (ROWS, HD), 0)
    lane = lax.broadcasted_iota(jnp.int32, (ROWS, HD), 1)
    lens = jnp.zeros((ROWS, HD), jnp.int32)
    for k in range(ROWS - 1):
        lens = jnp.where(sub == k + 1, len_ref[0, k], lens)
    allowed = (block * CACHE_BLOCK + lane < lens)[None]
    tiles = STEPS * 8
    small = lane % 32
    for head in range(2):
        key = slice(head * 256, head * 256 + HD)
        value = slice(head * 256 + HD, head * 256 + 256)
        q = jnp.concatenate(
            [
                q_ref[0, t, :, (head * 8 + g) * HD : (head * 8 + g + 1) * HD].astype(f32)
                for t in range(STEPS)
                for g in range(8)
            ],
            axis=0,
        ).astype(bf16)
        scores = jnp.zeros((tiles, ROWS, HD), f32)
        for k in range(0, ROWS - 1, 2):
            n = min(2, ROWS - 1 - k)
            part = dot_t(q, cache_ref[0, k : k + n, :, key].reshape(n * CACHE_BLOCK, HD))
            for e in range(n):
                one = part[:, e * HD : (e + 1) * HD].reshape(tiles, ROWS, HD)
                scores = jnp.where((sub == k + e + 1)[None], one, scores)
        scores = jnp.where(allowed, scores * FACTOR, NEG_FILL)
        peak = jnp.max(scores, axis=-1, keepdims=True)
        weights = jnp.where(allowed, jnp.exp(scores - peak), 0.0)
        totals = jnp.sum(weights, axis=-1, keepdims=True)
        wide = jnp.concatenate(
            [
                jnp.where((sub == k + 1)[None], weights, 0.0).reshape(tiles * ROWS, HD).astype(bf16)
                for k in range(ROWS - 1)
            ],
            axis=1,
        )
        values = cache_ref[0, :, :, value].reshape((ROWS - 1) * CACHE_BLOCK, HD)
        mix = dot(wide, values).reshape(STEPS, 8, ROWS, HD)
        peak = peak.reshape(STEPS, 8, ROWS, 1)
        totals = totals.reshape(STEPS, 8, ROWS, 1)
        for half in range(2):
            stats = jnp.zeros((ROWS, HD), f32)
            for t in range(STEPS):
                for h in range(4):
                    j = t * 4 + h
                    stats = jnp.where(small == j, peak[t, half * 4 + h], stats)
                    stats = jnp.where(small == 16 + j, totals[t, half * 4 + h], stats)
            high = stats.astype(bf16).astype(f32)
            rest = stats - high
            mid = rest.astype(bf16).astype(f32)
            low = rest - mid
            packed = jnp.where(lane < 32, high, jnp.where(lane < 64, mid, low))
            slot = head * 2 + half
            out_ref[slot, 0:128] = mix[:, half * 4 : half * 4 + 4].reshape(128, HD).astype(bf16)
            out_ref[slot, 128:144] = jnp.concatenate(
                [packed, jnp.zeros((ROWS, HD), f32)], axis=0
            ).astype(bf16)


def decode_parts(cache_lengths, decode_queries, kv_cache, after):
    return pl.pallas_call(
        decode_kernel,
        out_shape=jax.ShapeDtypeStruct((BLOCKS, PART_ROWS, HD), bf16),
        grid_spec=pltpu.PrefetchScalarGridSpec(
            num_scalar_prefetch=1,
            grid=(KVH // 2,),
            in_specs=[
                pl.BlockSpec((1, STEPS, ROWS, 2048), lambda c, *_: (0, 0, 0, c)),
                pl.BlockSpec((1, ROWS - 1, CACHE_BLOCK, 512), lambda c, *_: (0, 0, 0, c)),
                pl.BlockSpec(memory_space=pl.ANY),
            ],
            out_specs=pl.BlockSpec((4, PART_ROWS, HD), lambda c, *_: (c, 0, 0)),
        ),
        compiler_params=params(),
        cost_estimate=pl.CostEstimate(
            flops=2000000000, bytes_accessed=4800000, transcendentals=300000
        ),
        name="decode_parts",
    )(cache_lengths, decode_queries, kv_cache, after)


def prompt_kernel(index, heads, start_ref, q_ref, prefix_ref, own_ref, other_ref, *rest):
    out_ref, mixed, least = rest[-3:]
    side = lax.axis_index("side")
    start = start_ref[lax.axis_index("pair")]
    tokens = 256
    own_keys = (index + 1) * tokens
    scale = FACTOR * LOG2E

    pos = lax.broadcasted_iota(jnp.int32, (PREFIX, 2 * HD), 0)
    wide = jnp.concatenate([prefix_ref[0, :, HD:], jnp.ones((PREFIX, HD), bf16)], axis=1)
    mixed[SEG_HALF : SEG_HALF + PREFIX] = jnp.where(pos < start, wide.astype(f32), 0.0).astype(bf16)
    ones = jnp.ones((SEG_HALF, HD), bf16)
    mixed[:SEG_HALF] = jnp.concatenate([other_ref[0, :, HD:], ones], axis=1)
    mixed[SEG_HALF + PREFIX :] = jnp.concatenate([own_ref[0, :, HD:], ones], axis=1)
    least[...] = jnp.ones(least.shape, f32)

    def norm(ref):
        k = ref[0, :, :HD].astype(f32)
        return jnp.max(jnp.sum(k * k, axis=-1, keepdims=True), axis=0, keepdims=True)

    longest = jnp.maximum(norm(prefix_ref), jnp.maximum(norm(own_ref), norm(other_ref)))
    causal = lax.broadcasted_iota(jnp.int32, (tokens, tokens), 1) <= lax.broadcasted_iota(
        jnp.int32, (tokens, tokens), 0
    )

    def key_parts(later):
        parts = []
        if later:
            parts += [(other_ref, n) for n in range(0, SEG_HALF, 256)]
        parts += [(prefix_ref, n) for n in range(0, PREFIX, 256)]
        parts += [(own_ref, n) for n in range(0, own_keys, 256)]
        return parts

    def one_head(g, later):
        col = pl.ds(pl.multiple_of(g * HD, HD), HD)
        q = q_ref[0, :, col]
        wide_q = q.astype(f32)
        bound = jnp.sqrt(jnp.sum(wide_q * wide_q, axis=-1, keepdims=True) * longest) * scale
        parts = key_parts(later)
        weights = []
        for number, (ref, n) in enumerate(parts):
            w = jnp.exp2(dot_t(q, ref[0, n : n + 256, :HD]) * scale - bound)
            if number == len(parts) - 1:
                w = jnp.where(causal, w, 0.0)
            weights.append(w.astype(bf16))
        first = 0 if later else SEG_HALF
        total = dot(
            jnp.concatenate(weights, axis=1), mixed[first : SEG_HALF + PREFIX + own_keys]
        )
        sums = total[:, HD:]
        out_ref[0, :, col] = (total[:, :HD] / sums).astype(bf16)
        least[...] = jnp.minimum(least[...], sums)

    def one_head_exact(g, later):
        col = pl.ds(pl.multiple_of(g * HD, HD), HD)
        q = q_ref[0, :, col]
        parts = key_parts(later)
        scores = []
        for number, (ref, n) in enumerate(parts):
            s = dot_t(q, ref[0, n : n + 256, :HD])
            if ref is prefix_ref:
                at = n + lax.broadcasted_iota(jnp.int32, s.shape, 1)
                s = jnp.where(at < start, s, NEG_FILL)
            if number == len(parts) - 1:
                s = jnp.where(causal, s, NEG_FILL)
            scores.append(s)
        peak = functools.reduce(
            jnp.maximum, [jnp.max(s, axis=-1, keepdims=True) for s in scores]
        )
        weights = [jnp.exp2((s - peak) * scale).astype(bf16) for s in scores]
        first = 0 if later else SEG_HALF
        total = dot(
            jnp.concatenate(weights, axis=1), mixed[first : SEG_HALF + PREFIX + own_keys]
        )
        out_ref[0, :, col] = (total[:, :HD] / total[:, HD:]).astype(bf16)

    for later in (False, True):

        @pl.when(side == int(later))
        def _(later=later):
            @pl.loop(0, 8 // heads)
            def _(step):
                for e in range(heads):
                    one_head(step * heads + e, later)

            @pl.when(jnp.min(least[...]) < 1e-27)
            def _():
                @pl.loop(0, 8)
                def _(g):
                    one_head_exact(g, later)


def prompt_block(index, heads, starts, queries, prefix, own, other, prior, after):
    operands = [starts, queries, prefix, own, other]
    block = pl.BlockSpec((1, 256, 1024), lambda g, *_: (0, index, 0))
    in_specs = [block, whole(prefix.shape), whole(own.shape), whole(other.shape)]
    aliases = {}
    if prior is not None:
        operands += [prior, after]
        in_specs += [pl.BlockSpec(memory_space=pl.ANY)] * 2
        aliases = {5: 0}
    keys = PREFIX + SEG_HALF + (index + 1) * 256
    return pl.pallas_call(
        functools.partial(prompt_kernel, index, heads),
        out_shape=jax.ShapeDtypeStruct(queries.shape, bf16),
        grid_spec=pltpu.PrefetchScalarGridSpec(
            num_scalar_prefetch=1,
            grid=(1,),
            in_specs=in_specs,
            out_specs=block,
            scratch_shapes=[
                pltpu.VMEM((2 * SEG_HALF + PREFIX, 2 * HD), bf16),
                pltpu.VMEM((256, HD), f32),
            ],
        ),
        input_output_aliases=aliases,
        compiler_params=params(),
        cost_estimate=pl.CostEstimate(
            flops=2048 * keys * 128 * 8, bytes_accessed=2000000, transcendentals=2048 * keys
        ),
        name="prompt_block",
    )(*operands)


def first_row_kernel(match_ref, start_ref, moved_ref, prefix_ref, own_ref, other_ref, after_ref, out_ref):
    group = lax.axis_index("pair")
    target = match_ref[group]
    start = start_ref[group]
    q = moved_ref[target, 0:16]
    fresh = moved_ref[target, 16:32]
    wide = fresh.astype(f32)
    fresh_v = jnp.concatenate([wide[8:], wide[:8]], axis=0).astype(bf16)
    s0 = dot_t(q, prefix_ref[0, :, :HD])
    pos = lax.broadcasted_iota(jnp.int32, s0.shape, 1)
    s0 = jnp.where(pos < start, s0, NEG_FILL)
    s1 = dot_t(q, own_ref[0, :, :HD])
    s2 = dot_t(q, other_ref[0, :, :HD])
    s3 = dot_t(q, fresh)
    step = lax.broadcasted_iota(jnp.int32, s3.shape, 0) // 4
    pos = lax.broadcasted_iota(jnp.int32, s3.shape, 1)
    s3 = jnp.where(pos <= step, s3, NEG_FILL)
    scores = (s0, s1, s2, s3)
    values = (prefix_ref[0, :, HD:], own_ref[0, :, HD:], other_ref[0, :, HD:], fresh_v)
    peak = functools.reduce(jnp.maximum, [jnp.max(s, axis=-1, keepdims=True) for s in scores])
    mix = jnp.zeros((16, HD), f32)
    totals = jnp.zeros((16, 1), f32)
    for s, v in zip(scores, values):
        w = jnp.exp2((s - peak) * (FACTOR * LOG2E))
        totals += jnp.sum(w, axis=-1, keepdims=True)
        mix += dot(w.astype(bf16), v)
    out_ref[...] = jnp.zeros(out_ref.shape, bf16)
    out_ref[target] = (mix / totals).astype(bf16)


def first_row(matching, starts, moved, prefix, own, other, after):
    return pl.pallas_call(
        first_row_kernel,
        out_shape=jax.ShapeDtypeStruct((GROUPS, 16, HD), bf16),
        grid_spec=pltpu.PrefetchScalarGridSpec(
            num_scalar_prefetch=2,
            grid=(1,),
            in_specs=[whole(moved.shape), whole(prefix.shape), whole(own.shape), whole(other.shape)]
            + [pl.BlockSpec(memory_space=pl.ANY)],
            out_specs=whole((GROUPS, 16, HD)),
        ),
        compiler_params=params(),
        cost_estimate=pl.CostEstimate(
            flops=20000000, bytes_accessed=1300000, transcendentals=33000
        ),
        name="first_row",
    )(matching, starts, moved, prefix, own, other, after)


def merge_kernel(match_ref, parts_ref, first_ref, q_ref, kv_ref, out_ref):
    group = lax.axis_index("pair")
    block = lax.axis_index("side") * 8 + lax.axis_index("tp")
    source = jnp.int32(0)
    for p in range(GROUPS):
        source = jnp.where(match_ref[p] == group, p, source)
    q = q_ref[0, :, :, pl.ds(pl.multiple_of(block * 512, 512), 512)].astype(f32)
    kv = kv_ref[0, :, :, pl.ds(pl.multiple_of((block // 2) * 256, 256), 256)].astype(f32)
    sub = lax.broadcasted_iota(jnp.int32, (ROWS, HD), 0)
    lane = lax.broadcasted_iota(jnp.int32, (ROWS, HD), 1)

    peaks, totals = [], []
    for b in range(BLOCKS):
        x = parts_ref[b, 128:144].astype(f32)[:ROWS]
        x = x + pltpu.roll(x, HD - 32, 1) + pltpu.roll(x, HD - 64, 1)
        peaks.append(x)
        totals.append(pltpu.roll(x, HD - 16, 1))
    top = functools.reduce(jnp.maximum, peaks)
    fresh = {}
    fresh_top = jnp.full((ROWS, HD), NEG_FILL, f32)
    for t in range(STEPS):
        for h in range(4):
            j = t * 4 + h
            qt = q[t, :, h * HD : (h + 1) * HD]
            for u in range(t + 1):
                s = jnp.sum(qt * kv[u, :, :HD], axis=-1, keepdims=True) * FACTOR
                fresh[j, u] = s
                fresh_top = jnp.where(lane == j, jnp.maximum(fresh_top, s), fresh_top)
    top = jnp.maximum(top, fresh_top)
    scales = [jnp.exp(p - top) for p in peaks]
    total = functools.reduce(jnp.add, [s * t for s, t in zip(scales, totals)])
    first = first_ref[source].astype(f32)
    for t in range(STEPS):
        for h in range(4):
            j = t * 4 + h
            acc = jnp.zeros((ROWS, HD), f32)
            for b in range(0, BLOCKS):
                tile = parts_ref[b, (j // 2) * 16 : (j // 2) * 16 + 16].astype(f32)
                acc += scales[b][:, j : j + 1] * tile[(j % 2) * 8 : (j % 2) * 8 + 8]
            denom = total[:, j : j + 1]
            for u in range(t + 1):
                w = jnp.exp(fresh[j, u] - top[:, j : j + 1])
                acc += w * kv[u, :, HD:]
                denom = denom + w
            out = acc / denom
            out = jnp.where(sub == 0, first[j : j + 1], out)
            out_ref[0, t, :, h * HD : (h + 1) * HD] = out.astype(bf16)


def merge(matching, parts, first, decode_queries, decode_kv):
    shape = (1, STEPS, ROWS, 512)
    return pl.pallas_call(
        merge_kernel,
        out_shape=jax.ShapeDtypeStruct(shape, bf16),
        grid_spec=pltpu.PrefetchScalarGridSpec(
            num_scalar_prefetch=1,
            grid=(1,),
            in_specs=[
                whole(parts.shape),
                whole(first.shape),
                whole(decode_queries.shape),
                whole(decode_kv.shape),
            ],
            out_specs=whole(shape),
        ),
        compiler_params=params(),
        cost_estimate=pl.CostEstimate(flops=3000000, bytes_accessed=1300000, transcendentals=60000),
        name="merge",
    )(matching, parts, first, decode_queries, decode_kv)


def local(
    segment_queries,
    segment_kv,
    prefix_kv,
    kv_cache,
    decode_queries,
    decode_kv,
    matching,
    segment_starts,
    cache_lengths,
):
    other_kv = lax.ppermute(segment_kv, "side", [(0, 1), (1, 0)])
    moved = prep(decode_queries, decode_kv)
    moved = lax.all_to_all(moved, "pair", split_axis=0, concat_axis=0, tiled=True)
    keys = (prefix_kv, segment_kv, other_kv)
    out = prompt_block(0, 1, segment_starts, segment_queries, *keys, None, None)
    first = first_row(matching, segment_starts, moved, *keys, out)
    parts = decode_parts(cache_lengths, decode_queries, kv_cache, first)
    first = lax.all_to_all(first, "pair", split_axis=0, concat_axis=0, tiled=True)
    first = lax.ppermute(
        first, ("side", "tp"), [(s * 8 + c, 2 * c + s) for s in range(2) for c in range(8)]
    )
    out = prompt_block(1, 2, segment_starts, segment_queries, *keys, out, parts)
    parts = lax.all_to_all(parts, ("side", "tp"), split_axis=0, concat_axis=0, tiled=True)
    decode_out = merge(matching, parts, first, decode_queries, decode_kv)
    return (out, decode_out)


def solution(mesh):
    in_specs = (
        P("pair", "side", "tp"),
        P("pair", "side", "tp"),
        P("pair", None, "tp"),
        P("pair", None, ("side", "tp"), None),
        P("pair", None, None, None),
        P("pair", None, None, None),
        P(),
        P(),
        P("pair", None),
    )
    out_specs = (P("pair", "side", "tp"), P("pair", None, None, ("side", "tp")))
    return jax.shard_map(local, mesh=mesh, in_specs=in_specs, out_specs=out_specs, check_vma=False)
```

time: 457 us -> 83.7 us (0.18)
  waiting for transfers between devices: 182 us -> 0.01 us
  blocking collectives: 149 us -> 0 us
  Pallas kernels: 0 us -> 54.6 us
  matrix products: 34.3 us -> 0 us
  local copies, waits for them, and re-layouts: 35.6 us -> 2.76 us
  other arithmetic: 32.5 us -> 0 us
  starting transfers between devices: 1.37 us -> 25.5 us
  between operations: 16.5 us -> 0.66 us
    all_gather x1 -> x0, waiting for transfers between devices: 157 us -> none  [local(): pieces = lax.all_gather(blocks_kv[None], 'pair', axis=0, tiled=True)]
    pmax x1 -> x0, blocking collectives: 69 us -> none  [local(): highest = lax.pmax(local_peak, ('side', 'tp'))]
    psum x1 -> x0, blocking collectives: 65.3 us -> none  [local(): totals, mixture = lax.psum((totals, mixture), ('side', 'tp'))]
    pallas_call x0 -> x6, Pallas kernels: none -> 54.6 us  [the longest x2 39.6 us: prompt_block(): pl.pallas_call(functools.partial(prompt_kernel, index, heads), out_shape=...]
    dot_general x8 -> x0, matrix products: 34.3 us -> none  [the longest x2 14.9 us: prompt_block(): jnp.einsum('qcgd,jcd->qcgj', queries, keys_all[:, :, 0], preferred_elemen...]
    reduce_sum x6 -> x0, other arithmetic: 26.4 us -> none  [the longest x4 20.7 us: softmax_parts(): return (weights.astype(jnp.bfloat16), jnp.sum(weights, axis=-1))]
    psum x1 -> x0, waiting for transfers between devices: 25.2 us -> none  [local(): totals, mixture = lax.psum((totals, mixture), ('side', 'tp'))]
    all_to_all x0 -> x3, starting transfers between devices: none -> 19.9 us  [the longest x1 8.95 us: local(): lax.all_to_all(moved, 'pair', split_axis=0, concat_axis=0, tiled=True)]
  transfers between devices with their start and end apart: 3 -> 5, of which waited for: 2 -> 0; matrix products, arithmetic and copies ran while one was open for 18% -> 0% of each run, Pallas kernels for 0% -> 58%
where the time goes in v1:
time: 83.7 us; the launch traced here: 83.6 us
  Pallas kernels  54.6 us (65%)
  starting transfers between devices  25.5 us (30%)
  local copies, waits for them, and re-layouts  2.76 us (3%)
    pallas_call x2, Pallas kernels, prompt_block(): pl.pallas_call(functools.partial(prompt_kernel, index, heads), out_shape=...  39.6 us
    all_to_all x1, starting transfers between devices, local(): lax.all_to_all(moved, 'pair', split_axis=0, concat_axis=0, tiled=True)  8.95 us
    pallas_call x1, Pallas kernels, decode_parts(): pl.pallas_call(decode_kernel, out_shape=jax.ShapeDtypeStruct((BLOCKS, PAR...  7.04 us
    all_to_all x1, starting transfers between devices, local(): lax.all_to_all(first, 'pair', split_axis=0, concat_axis=0, tiled=True)  6.67 us
    ppermute x1, starting transfers between devices, local(): lax.ppermute(first, ('side', 'tp'), [(s * 8 + c, 2 * c + s) for s in rang...  4.88 us
    all_to_all x1, starting transfers between devices, local(): lax.all_to_all(parts, ('side', 'tp'), split_axis=0, concat_axis=0, tiled=...  4.28 us
    pallas_call x1, Pallas kernels, merge(): pl.pallas_call(merge_kernel, out_shape=jax.ShapeDtypeStruct(shape, bf16),...  3.2 us
    pallas_call x1, Pallas kernels, first_row(): pl.pallas_call(first_row_kernel, out_shape=jax.ShapeDtypeStruct((GROUPS,...  3.03 us
  transfers between devices with their start and end apart: 5, of which 0 were waited for; matrix products, arithmetic and copies ran while one was open for 0% of the time, Pallas kernels for 58%

profile of v1, /device:TPU:57, one launch (start us, length us, event | category | flops | bytes accessed | tf_op | source)
XLA Modules:
  0.0 83.6 jit_solution(15960630677510821781)
XLA Ops:
  0.6 0.8 collective-permute-start
  1.4 1.7 %prep.1 = bf16[16,32,128]{2,1,0:T(8,128)(2,1)} custom-call(bf16[1,4,8,8192]{3,2,1,0:T(8,128)(2,1)} %q_ref.9, bf16[1,4,8,2048]{3,2,1,0:T(8,128)(2,1)} %kv_ref.3), custom_call_target="tpu_custom_call" | custom-call | flops 10000 | bytes 800000 | tf_op jit(solution)/shard_map/prep/pallas_call | solution.py:65
  3.1 9.0 %all-to-all-start = ((bf16[16,32,128]{2,1,0:T(8,128)(2,1)}), bf16[16,32,128]{2,1,0:T(8,128)(2,1)S(1)}, u32[]{:S(2)}, u32[]{:S(2)}) async-start(bf16[16,32,128]{2,1,0:T(8,128)(2,1)} %prep.1), calls=%async_computation | async-start | bytes 262144 | tf_op jit(solution)/shard_map/all_to_all | solution.py:418
  12.1 0.0 collective-permute-done.other_ref
  12.1 0.0 copy-start.2
  12.1 0.7 copy-done.2
  12.8 19.5 %prompt_block.2.after_ref.rest_0_ = bf16[1,512,1024]{2,1,0:T(8,128)(2,1)} custom-call(s32[16]{0:T(128)} %start_ref.5, bf16[1,512,1024]{2,1,0:T(8,128)(2,1)} %q_ref.8, bf16[1,1024,256]{2,1,0:T(8,128)(2,1)} %prefix_ref.5, bf16[1,512,256]{2,1,0:T(8,128)(2,1)} %own_ref.5, bf16[1,512,256]{2,1,0:T(8,128)(2,1)} %copy-done.2), custom_call_target="tpu_custom_call" | custom-call | flops 3758096384 | bytes 2000000 | tf_op jit(solution)/shard_map/prompt_block/pallas_call | solution.py:263
  32.3 0.0 all-to-all-done.moved_ref
  32.3 0.0 copy-start.1
  32.3 0.6 copy-done.1
  33.0 3.0 %first_row.1.after_ref = bf16[16,16,128]{2,1,0:T(8,128)(2,1)} custom-call(s32[16]{0:T(128)} %match_ref.3, s32[16]{0:T(128)} %start_ref.5, bf16[16,32,128]{2,1,0:T(8,128)(2,1)} %copy-done.1, bf16[1,1024,256]{2,1,0:T(8,128)(2,1)} %prefix_ref.5, bf16[1,512,256]{2,1,0:T(8,128)(2,1)} %own_ref.5, bf16[1,512,256]{2,1,0:T(8,128)(2,1)} %copy-done.2, ...), custom_call_target="tpu_custom_call" | custom-call | flops 20000000 | bytes 1300000 | tf_op jit(solution)/shard_map/first_row/pallas_call | solution.py:316
  36.0 6.7 %all-to-all-start.2 = ((bf16[16,16,128]{2,1,0:T(8,128)(2,1)}), bf16[16,16,128]{2,1,0:T(8,128)(2,1)S(1)}, u32[]{:S(2)}, u32[]{:S(2)}) async-start(bf16[16,16,128]{2,1,0:T(8,128)(2,1)} %first_row.1.after_ref), calls=%async_computation.2 | async-start | bytes 131072 | tf_op jit(solution)/shard_map/all_to_all | solution.py:423
  42.6 7.0 %decode_parts.1.rest_1_ = bf16[16,144,128]{2,1,0:T(8,128)(2,1)} custom-call(s32[1,7]{1,0:T(1,128)} %len_ref.1, bf16[1,4,8,8192]{3,2,1,0:T(8,128)(2,1)} %q_ref.9, bf16[1,7,128,2048]{3,2,1,0:T(8,128)(2,1)} %cache_ref.1, bf16[16,16,128]{2,1,0:T(8,128)(2,1)} %first_row.1.after_ref), custom_call_target="tpu_custom_call" | custom-call | flops 2000000000 | bytes 4800000 | tf_op jit(solution)/shard_map/decode_parts/pallas_call | solution.py:140
  49.7 0.0 all-to-all-done.2
  49.7 4.3 %all-to-all-start.1 = ((bf16[16,144,128]{2,1,0:T(8,128)(2,1)}), bf16[16,144,128]{2,1,0:T(8,128)(2,1)S(1)}, u32[]{:S(2)}, u32[]{:S(2)}) async-start(bf16[16,144,128]{2,1,0:T(8,128)(2,1)} %decode_parts.1.rest_1_), calls=%async_computation.1 | async-start | bytes 1179648 | tf_op jit(solution)/shard_map/all_to_all | solution.py:428
  54.0 4.9 %collective-permute-start.1 = (bf16[16,16,128]{2,1,0:T(8,128)(2,1)S(1)}, bf16[16,16,128]{2,1,0:T(8,128)(2,1)S(1)}, u32[]{:S(2)}, u32[]{:S(2)}) collective-permute-start(bf16[16,16,128]{2,1,0:T(8,128)(2,1)S(1)} %all-to-all-done.2), channel_id=1, source_target_pairs={{0,0},{1,2},{2,4},{3,6},{4,8},{5,10},{6,12},{7,14},{8,1},{9,3},{10... | collective-permute-start | bytes 196616 | tf_op jit(solution)/shard_map/ppermute | solution.py:424
  58.9 20.1 %prompt_block.3 = bf16[1,512,1024]{2,1,0:T(8,128)(2,1)} custom-call(s32[16]{0:T(128)} %start_ref.5, bf16[1,512,1024]{2,1,0:T(8,128)(2,1)} %q_ref.8, bf16[1,1024,256]{2,1,0:T(8,128)(2,1)} %prefix_ref.5, bf16[1,512,256]{2,1,0:T(8,128)(2,1)} %own_ref.5, bf16[1,512,256]{2,1,0:T(8,128)(2,1)} %copy-done.2, ...), custom_call_target="tpu_custom_call", output_to_operand_aliasing={{}: (5, {})} | custom-call | flops 4294967296 | bytes 2000000 | tf_op jit(solution)/shard_map/prompt_block/pallas_call | solution.py:263
  78.9 0.0 collective-permute-done.1.first_ref
  78.9 0.0 copy-start.3
  78.9 0.0 all-to-all-done.1.parts_ref
  78.9 0.6 copy-done.3
  79.6 0.0 copy-start
  79.6 0.8 copy-done
  80.4 3.2 %merge.1 = bf16[1,4,8,512]{3,2,1,0:T(8,128)(2,1)} custom-call(s32[16]{0:T(128)} %match_ref.3, bf16[16,144,128]{2,1,0:T(8,128)(2,1)} %copy-done, bf16[16,16,128]{2,1,0:T(8,128)(2,1)} %copy-done.3, bf16[1,4,8,8192]{3,2,1,0:T(8,128)(2,1)} %q_ref.9, bf16[1,4,8,2048]{3,2,1,0:T(8,128)(2,1)} %kv_ref.3), custom_call_target="tpu_custom_call" | custom-call | flops 3000000 | bytes 1300000 | tf_op jit(solution)/shard_map/merge/pallas_call | solution.py:385
Async XLA Ops:
  0.6 11.4 %collective-permute-start = (bf16[1,512,256]{2,1,0:T(8,128)(2,1)}, bf16[1,512,256]{2,1,0:T(8,128)(2,1)S(1)}, u32[]{:S(2)}, u32[]{:S(2)}) collective-permute-start(bf16[1,512,256]{2,1,0:T(8,128)(2,1)} %own_ref.5), channel_id=1, source_target_pairs={{0,8},{8,0},{1,9},{9,1},{2,10},{10,2},{3,11},{11,3},{4,12},{12,4},... | collective-permute-start | bytes 786440 | tf_op jit(solution)/shard_map/ppermute | solution.py:416
  3.1 29.2 %all-to-all-start = ((bf16[16,32,128]{2,1,0:T(8,128)(2,1)}), bf16[16,32,128]{2,1,0:T(8,128)(2,1)S(1)}, u32[]{:S(2)}, u32[]{:S(2)}) async-start(bf16[16,32,128]{2,1,0:T(8,128)(2,1)} %prep.1), calls=%async_computation | async-start | bytes 262144 | tf_op jit(solution)/shard_map/all_to_all | solution.py:418
  12.1 0.7 copy-start.2
  32.3 0.6 copy-start.1
  36.0 13.7 %all-to-all-start.2 = ((bf16[16,16,128]{2,1,0:T(8,128)(2,1)}), bf16[16,16,128]{2,1,0:T(8,128)(2,1)S(1)}, u32[]{:S(2)}, u32[]{:S(2)}) async-start(bf16[16,16,128]{2,1,0:T(8,128)(2,1)} %first_row.1.after_ref), calls=%async_computation.2 | async-start | bytes 131072 | tf_op jit(solution)/shard_map/all_to_all | solution.py:423
  49.7 29.3 %all-to-all-start.1 = ((bf16[16,144,128]{2,1,0:T(8,128)(2,1)}), bf16[16,144,128]{2,1,0:T(8,128)(2,1)S(1)}, u32[]{:S(2)}, u32[]{:S(2)}) async-start(bf16[16,144,128]{2,1,0:T(8,128)(2,1)} %decode_parts.1.rest_1_), calls=%async_computation.1 | async-start | bytes 1179648 | tf_op jit(solution)/shard_map/all_to_all | solution.py:428
  54.0 25.0 %collective-permute-start.1 = (bf16[16,16,128]{2,1,0:T(8,128)(2,1)S(1)}, bf16[16,16,128]{2,1,0:T(8,128)(2,1)S(1)}, u32[]{:S(2)}, u32[]{:S(2)}) collective-permute-start(bf16[16,16,128]{2,1,0:T(8,128)(2,1)S(1)} %all-to-all-done.2), channel_id=1, source_target_pairs={{0,0},{1,2},{2,4},{3,6},{4,8},{5,10},{6,12},{7,14},{8,1},{9,3},{10... | collective-permute-start | bytes 196616 | tf_op jit(solution)/shard_map/ppermute | solution.py:424
  78.9 0.6 copy-start.3
  79.6 0.8 copy-start
